TPU v7x, 256 devices: a whole 4x4x8 slice. The times are simulated.
256 devices in a mesh: sub: 64 (over y, z, core), grp: 4 (over x).
Axes of the slice: x: 4, y: 4, z: 8, core: 2. Of those that a mesh axis runs over, the one named last changes fastest.
Arguments:
- interface_values: float32 [4, 64, 16, 128], P('grp', 'sub'), may hold values from 0.1 to 10
- send_blocks: int32 [4, 64, 4, 8], P('grp', 'sub'), may hold values from 0 to 15
- recv_blocks: int32 [4, 64, 4, 8], P('grp', 'sub'), may hold values from 0 to 15
- block_counts: int32 [4, 64, 4], P('grp', 'sub'), may hold values from 1 to 8, as said below
- live_sizes: int32 [4, 64], P('grp', 'sub'), may hold values from 1 to 2048, 43690 in all within a row
- schur: bfloat16 [4, 64, 2048, 2048], P('grp', 'sub'), may hold values from -0.125 to 0.125
- basis: bfloat16 [4, 64, 96, 2048], P('grp', 'sub'), may hold values from -6 to 6
- coarse_map: int32 [4, 64, 96], P('grp'), may hold values from 0 to 1023, as said below
Outputs:
- weights: float32 [4, 64, 16, 128], P('grp', 'sub')
- schur_image: bfloat16 [4, 64, 96, 2048], P('grp', 'sub')
- coarse: float32 [4, 1024, 1024], P('grp', 'sub')
Inputs may be any that keep to these rules, and one draw needn't show every extreme that they name: `block_counts`: toward direction 0 some subdomain of each group fills all 8 slots. `live_sizes`: within one group the live sizes sum to 43690, and the largest is 2048. `coarse_map`: the 96 coarse unknowns of one subdomain are distinct.
All inputs are finite; a program needn't handle non-finite values.
Results may differ from a plain program's by a relative error of at most 0.0042.
Values may be sent and summed in bfloat16 or wider, within the bound.
A program may use at most 64 MiB of HBM per device.

v0:
```python
import jax
import jax.numpy as jnp
from jax import lax
from jax.sharding import PartitionSpec as P

CROWS = 16


def extended(block, sides, width, periodic):
    for axis, dim in sides:
        count = lax.axis_size(axis)
        forward = [(i, i + 1) for i in range(count - 1)]
        if periodic:
            forward.append((count - 1, 0))
        backward = [(target, source) for source, target in forward]
        low = lax.ppermute(
            lax.slice_in_dim(block, block.shape[dim] - width, None, axis=dim), axis, forward
        )
        high = lax.ppermute(lax.slice_in_dim(block, 0, width, axis=dim), axis, backward)
        block = jnp.concatenate([low, block, high], axis=dim)
    return block


def shards(
    interface_values, send_blocks, recv_blocks, block_counts, live_sizes, schur, basis, coarse_map
):
    values = interface_values[0, 0]
    block_count, block_rows = values.shape
    slot_count = send_blocks.shape[3]
    blocks = jnp.arange(block_count)
    chosen = (send_blocks[0, 0][..., None] == blocks).astype(jnp.float32)
    filled = (jnp.arange(slot_count)[None, :] < block_counts[0, 0][:, None]).astype(jnp.float32)
    packed = (
        jnp.einsum("jfn,nb->jfb", chosen, values, precision=lax.Precision.HIGHEST)
        * filled[:, :, None]
    )
    along_sub = extended(jnp.stack([packed[1], packed[0]]), (("sub", 0),), 1, True)
    along_grp = extended(jnp.stack([packed[3], packed[2]]), (("grp", 0),), 1, False)
    arrived = jnp.stack([along_sub[0], along_sub[3], along_grp[0], along_grp[3]])
    placed = (recv_blocks[0, 0][..., None] == blocks).astype(jnp.float32)
    totals = values + jnp.einsum("jfn,jfb->nb", placed, arrived, precision=lax.Precision.HIGHEST)
    weights = values / totals
    interface = block_count * block_rows
    live_size = live_sizes[0, 0]
    live_mask = (jnp.arange(interface) < live_size).astype(jnp.float32)
    primal_basis = basis[0, 0]
    scaled = (
        primal_basis.astype(jnp.float32) * (weights.reshape(interface) * live_mask)[None, :]
    ).astype(jnp.bfloat16)
    matrix = schur[0, 0]
    images = lax.dot_general(
        scaled, matrix, (((1,), (1,)), ((), ())), preferred_element_type=jnp.float32
    )
    images = images * live_mask[None, :]
    partial_value = (
        lax.dot_general(
            scaled.astype(jnp.float32),
            images,
            (((1,), (1,)), ((), ())),
            precision=lax.Precision.HIGHEST,
        )
        / interface
    )
    partial_value = partial_value.astype(jnp.bfloat16)
    owner_map = coarse_map[0]
    section = CROWS * lax.axis_size("sub")
    my_map = lax.dynamic_index_in_dim(owner_map, lax.axis_index("sub"), 0, keepdims=False)
    col_pick = (my_map[:, None] == jnp.arange(section)[None, :]).astype(jnp.float32)
    right_side = jnp.dot(
        partial_value.astype(jnp.float32), col_pick, precision=lax.Precision.HIGHEST
    )
    row_pick = (my_map[:, None] == jnp.arange(lax.axis_size("sub") * CROWS)[None, :]).astype(
        jnp.float32
    )
    coarse = lax.psum_scatter(
        lax.dot_general(
            row_pick, right_side, (((0,), (0,)), ((), ())), precision=lax.Precision.HIGHEST
        ),
        "sub",
        scatter_dimension=0,
        tiled=True,
    )
    return (weights[None, None], images.astype(jnp.bfloat16)[None, None], coarse[None])


def solution(mesh):
    placed = (
        P("grp", "sub", None, None),
        P("grp", "sub", None, None),
        P("grp", "sub", None, None),
        P("grp", "sub", None),
        P("grp", "sub"),
        P("grp", "sub", None, None),
        P("grp", "sub", None, None),
        P("grp", None, None),
    )
    return jax.shard_map(
        shards,
        mesh=mesh,
        in_specs=placed,
        out_specs=(P("grp", "sub", None, None), P("grp", "sub", None, None), P("grp", "sub", None)),
        check_vma=False,
    )
```

profile of v0, /device:TPU:2, one launch (start us, length us, event | category | flops | bytes accessed | tf_op | source)
XLA Modules:
  0.0 185.4 jit_solution(16950739709942389540)
XLA Ops:
  7.2 0.0 copy-start
  7.2 0.0 copy-start.1
  7.2 0.0 reduce-scatter.2.cloned.1.call-start
  7.2 0.8 fusion.31
  8.0 0.9 convolution_multiply_fusion.1
  8.9 0.1 collective-permute-start
  9.0 4.2 %collective-permute-start.3 = (f32[1,8,128]{2,1,0:T(8,128)S(1)}, f32[1,8,128]{2,1,0:T(8,128)S(1)}, u32[]{:S(2)}, u32[]{:S(2)}) collective-permute-start(f32[1,8,128]{2,1,0:T(8,128)S(1)} %get-tuple-element.4), channel_id=1, source_target_pairs={{1,0},{2,1},{3,2},{5,4},{6,5},{7,6},{9,8},{10,9},{11,10},{13,12},{... | collective-permute-start | bytes 12296 | tf_op jit(solution)/shard_map/ppermute | solution.py:19
  13.2 1.9 %collective-permute-start.2 = (f32[1,8,128]{2,1,0:T(8,128)S(1)}, f32[1,8,128]{2,1,0:T(8,128)S(1)}, u32[]{:S(2)}, u32[]{:S(2)}) collective-permute-start(f32[1,8,128]{2,1,0:T(8,128)S(1)} %get-tuple-element.5), channel_id=1, source_target_pairs={{0,1},{1,2},{2,3},{4,5},{5,6},{6,7},{8,9},{9,10},{10,11},{12,13},{... | collective-permute-start | bytes 12296 | tf_op jit(solution)/shard_map/ppermute | solution.py:16
  15.1 7.0 %collective-permute-start.1 = (f32[1,8,128]{2,1,0:T(8,128)S(1)}, f32[1,8,128]{2,1,0:T(8,128)S(1)}, u32[]{:S(2)}, u32[]{:S(2)}) collective-permute-start(f32[1,8,128]{2,1,0:T(8,128)S(1)} %get-tuple-element.6), channel_id=1, source_target_pairs={{4,0},{8,4},{12,8},{16,12},{20,16},{24,20},{28,24},{32,28},{36,32}... | collective-permute-start | bytes 12296 | tf_op jit(solution)/shard_map/ppermute | solution.py:19
  22.8 0.0 copy-done
  22.8 0.0 collective-permute-done
  22.8 0.0 collective-permute-done.3
  22.9 0.0 collective-permute-done.2
  22.9 0.6 collective-permute-done.1
  23.5 1.6 bitcast_select_fusion
  25.1 6.2 %fusion.2 = f32[96,2048]{1,0:T(8,128)S(1)} fusion(bf16[1,1,2048,2048]{3,2,1,0:T(8,128)(2,1)} %param.13, bf16[1,1,96,2048]{3,2,1,0:T(8,128)(2,1)} %param.14, f32[2048]{0:T(1024)S(1)} %fusion.28, f32[2048]{0:T(1024)S(1)} %get-tuple-element.7), kind=kOutput, calls=%fused_computation.2 | convolution fusion | flops 806092800 | bytes 9584640 | tf_op jit(solution)/shard_map/dot_general | solution.py:51
  31.3 0.0 copy-done.1
  31.3 0.6 fusion.5
  31.9 0.3 fusion.16
  32.2 3.8 %fusion.15 = f32[1024,1024]{1,0:T(8,128)} fusion(f32[96,1024]{1,0:T(8,128)S(1)} %fusion.16, s32[96]{0:T(128)S(1)} %dynamic-slice_bitcast_fusion), kind=kOutput, calls=%fused_computation.17 | convolution fusion | flops 1208057856 | bytes 4587904 | tf_op jit(solution)/shard_map/dot_general | solution.py:76
  36.0 0.0 reduce-scatter.2.cloned.1.call-update
  36.0 0.8 convert_bitcast_fusion.1
  36.8 141.8 %reduce-scatter.2.cloned.1.call-done = f32[16,1024]{1,0:T(8,128)} async-done(((f32[1024,1024]{1,0:T(8,128)}), f32[16,1024]{1,0:T(8,128)}) %reduce-scatter.2.cloned.1.call-update) | async-done | bytes 65552 | tf_op jit(solution)/shard_map/reduce_scatter | solution.py:75
  (3 shorter events, 0.0 us)
Async XLA Ops:
  7.2 15.6 %copy-start = (s32[1,64,96]{2,1,0:T(8,128)S(1)}, s32[1,64,96]{2,1,0:T(8,128)}, u32[]{:S(2)}) copy-start(s32[1,64,96]{2,1,0:T(8,128)} %param.15) | copy-start | bytes 73732
  7.2 24.1 %copy-start.1 = (bf16[1,1,96,2048]{3,2,1,0:T(8,128)(2,1)S(1)}, bf16[1,1,96,2048]{3,2,1,0:T(8,128)(2,1)}, u32[]{:S(2)}) copy-start(bf16[1,1,96,2048]{3,2,1,0:T(8,128)(2,1)} %param.14) | copy-start | bytes 1179652
  7.2 171.4 %reduce-scatter.2.cloned.1.call-start = ((), (), s32[]{:S(2)}) async-start(), calls=%async_computation.1 | async-start | bytes 4259840 | tf_op jit(solution)/shard_map/reduce_scatter | solution.py:75
  8.9 13.9 %collective-permute-start = (f32[1,8,128]{2,1,0:T(8,128)S(1)}, f32[1,8,128]{2,1,0:T(8,128)S(1)}, u32[]{:S(2)}, u32[]{:S(2)}) collective-permute-start(f32[1,8,128]{2,1,0:T(8,128)S(1)} %get-tuple-element.3), channel_id=1, source_target_pairs={{0,4},{4,8},{8,12},{12,16},{16,20},{20,24},{24,28},{28,32},{32,36}... | collective-permute-start | bytes 12296 | tf_op jit(solution)/shard_map/ppermute | solution.py:16
  9.0 13.8 %collective-permute-start.3 = (f32[1,8,128]{2,1,0:T(8,128)S(1)}, f32[1,8,128]{2,1,0:T(8,128)S(1)}, u32[]{:S(2)}, u32[]{:S(2)}) collective-permute-start(f32[1,8,128]{2,1,0:T(8,128)S(1)} %get-tuple-element.4), channel_id=1, source_target_pairs={{1,0},{2,1},{3,2},{5,4},{6,5},{7,6},{9,8},{10,9},{11,10},{13,12},{... | collective-permute-start | bytes 12296 | tf_op jit(solution)/shard_map/ppermute | solution.py:19
  13.2 9.7 %collective-permute-start.2 = (f32[1,8,128]{2,1,0:T(8,128)S(1)}, f32[1,8,128]{2,1,0:T(8,128)S(1)}, u32[]{:S(2)}, u32[]{:S(2)}) collective-permute-start(f32[1,8,128]{2,1,0:T(8,128)S(1)} %get-tuple-element.5), channel_id=1, source_target_pairs={{0,1},{1,2},{2,3},{4,5},{5,6},{6,7},{8,9},{9,10},{10,11},{12,13},{... | collective-permute-start | bytes 12296 | tf_op jit(solution)/shard_map/ppermute | solution.py:16
  15.1 8.3 %collective-permute-start.1 = (f32[1,8,128]{2,1,0:T(8,128)S(1)}, f32[1,8,128]{2,1,0:T(8,128)S(1)}, u32[]{:S(2)}, u32[]{:S(2)}) collective-permute-start(f32[1,8,128]{2,1,0:T(8,128)S(1)} %get-tuple-element.6), channel_id=1, source_target_pairs={{4,0},{8,4},{12,8},{16,12},{20,16},{24,20},{28,24},{32,28},{36,32}... | collective-permute-start | bytes 12296 | tf_op jit(solution)/shard_map/ppermute | solution.py:19
Sparse Core Ops, SparseCore 0:
  36.1 142.3 reduce-scatter.1
where the time goes:
time: 186 us; the launch traced here: 185 us
  waiting for transfers between devices  142 us (76%)
  between operations  14.8 us (8%)
  matrix products  13.4 us (7%)
  starting transfers between devices  13.2 us (7%)
    reduce_scatter x1, waiting for transfers between devices, shards(): lax.psum_scatter(lax.dot_general(row_pick, right_side, (((0,), (0,)), (()...  142 us
    ppermute x2, starting transfers between devices, extended(): lax.ppermute(lax.slice_in_dim(block, 0, width, axis=dim), axis, backward)  11.2 us
    dot_general x1, matrix products, shards(): lax.dot_general(scaled, matrix, (((1,), (1,)), ((), ())), preferred_eleme...  6.24 us
    dot_general x1, matrix products, shards(): lax.dot_general(row_pick, right_side, (((0,), (0,)), ((), ())), precision...  3.84 us
  transfers between devices with their start and end apart: 5, of which 2 were waited for; matrix products, arithmetic and copies ran while one was open for 0% of the time, Pallas kernels for 0%

commit v1 on v0

v1 whole, which is shorter than its diff:
```python
import functools

import jax
import jax.numpy as jnp
from jax import lax
from jax.experimental import pallas as pl
from jax.experimental.pallas import tpu as pltpu
from jax.sharding import PartitionSpec as P

MESH = pl.DeviceIdType.MESH
LANES = 128
TILE = 256


def nt(left, right):
    return lax.dot_general(
        left, right, (((1,), (1,)), ((), ())), preferred_element_type=jnp.float32
    )


def nn(left, right):
    return lax.dot_general(
        left, right, (((1,), (0,)), ((), ())), preferred_element_type=jnp.float32
    )


def kernel(
    n_sub,
    n_grp,
    send_s,
    recv_s,
    counts_s,
    live_s,
    values_h,
    schur_h,
    basis_h,
    map_h,
    weights_h,
    image_h,
    coarse_h,
    values,
    basis,
    schur,
    cmap,
    packed,
    arrived,
    weights,
    scaled,
    image,
    part,
    row_pick,
    outgoing,
    incoming,
    high_pick,
    low_pick,
    spread,
    coarse,
    load_sem,
    schur_sem,
    store_sem,
    near_send,
    near_recv,
    far_send,
    far_recv,
):
    me = lax.axis_index("sub")
    group = lax.axis_index("grp")
    interface = schur.shape[0]
    columns = basis.shape[0]
    blocks = values.shape[0]
    rows = incoming.shape[1]
    section = rows * n_sub
    highs = section // LANES

    loads = [
        pltpu.make_async_copy(values_h.at[0, 0], values, load_sem.at[0]),
        pltpu.make_async_copy(map_h.at[0], cmap, load_sem.at[1]),
        pltpu.make_async_copy(basis_h.at[0, 0], basis, load_sem.at[2]),
    ]
    for load in loads:
        load.start()

    barrier = pltpu.get_barrier_semaphore()
    up = lax.rem(group + 1, n_grp)
    down = lax.rem(group + n_grp - 1, n_grp)
    pl.semaphore_signal(barrier, inc=1, device_id={"grp": up}, device_id_type=MESH)
    pl.semaphore_signal(barrier, inc=1, device_id={"grp": down}, device_id_type=MESH)

    def greet(step, carry):
        peer = lax.rem(me + step, n_sub)
        pl.semaphore_signal(barrier, inc=1, device_id={"sub": peer}, device_id_type=MESH)
        return carry

    lax.fori_loop(1, n_sub, greet, 0)

    tiles = interface // TILE
    schur_loads = [
        pltpu.make_async_copy(
            schur_h.at[0, 0, pl.ds(t * TILE, TILE)],
            schur.at[pl.ds(t * TILE, TILE)],
            schur_sem.at[t],
        )
        for t in range(tiles)
    ]
    for load in schur_loads:
        load.start()

    loads[0].wait()
    slots = packed.shape[1]
    for j in range(4):
        for f in range(slots):
            row = values[pl.ds(send_s[0, 0, j, f], 1), :]
            packed[j, f : f + 1, :] = jnp.where(f < counts_s[0, 0, j], row, 0.0)

    pl.semaphore_wait(barrier, n_sub + 1)

    right = lax.rem(me + 1, n_sub)
    left = lax.rem(me + n_sub - 1, n_sub)
    targets = [{"sub": right}, {"sub": left}, {"grp": up}, {"grp": down}]
    near = [
        pltpu.make_async_remote_copy(
            src_ref=packed.at[j],
            dst_ref=arrived.at[j],
            send_sem=near_send.at[j],
            recv_sem=near_recv.at[j],
            device_id=targets[j],
            device_id_type=MESH,
        )
        for j in range(4)
    ]
    for copy in near:
        copy.start()

    loads[1].wait()
    mine = cmap[pl.ds(me, 1), :]
    row_at = lax.broadcasted_iota(jnp.int32, (section, columns), 0)
    row_pick[...] = jnp.where(row_at == mine, 1.0, 0.0).astype(jnp.bfloat16)

    pad = jnp.full((1, LANES - columns), -1, jnp.int32)
    high_at = lax.broadcasted_iota(jnp.int32, (highs * rows, LANES), 0) // rows
    low_at = lax.broadcasted_iota(jnp.int32, (LANES, LANES), 0)

    def low(i, carry):
        row = jnp.concatenate([cmap[pl.ds(i, 1), :], pad], axis=1)
        at = pl.ds(pl.multiple_of(i * LANES, LANES), LANES)
        low_pick[:, at] = jnp.where(low_at == (row & (LANES - 1)), 1.0, 0.0).astype(jnp.bfloat16)
        return carry

    lax.fori_loop(0, n_sub, low, 0)
    part[...] = jnp.zeros_like(part)

    for copy in near:
        copy.wait()
    own = values[...]
    totals = own
    block_at = lax.broadcasted_iota(jnp.int32, own.shape, 0)
    for j in range(4):
        came = arrived[j]
        if j == 2:
            came = jnp.where(group > 0, came, 0.0)
        if j == 3:
            came = jnp.where(group < n_grp - 1, came, 0.0)
        for f in range(slots):
            totals += jnp.where(block_at == recv_s[0, 0, j, f], came[f : f + 1, :], 0.0)
    weight = own / totals
    weights[...] = weight
    weights_out = pltpu.make_async_copy(weights, weights_h.at[0, 0], store_sem.at[0])
    weights_out.start()

    live_size = live_s[0, 0]
    unknown = block_at * LANES + lax.broadcasted_iota(jnp.int32, own.shape, 1)
    live_weight = jnp.where(unknown < live_size, weight, 0.0)
    loads[2].wait()
    for n in range(blocks):
        at = slice(n * LANES, (n + 1) * LANES)
        scaled[:, at] = (basis[:, at].astype(jnp.float32) * live_weight[n : n + 1, :]).astype(
            jnp.bfloat16
        )

    total = jnp.zeros((columns, columns), jnp.float32)
    for t in range(tiles):
        at = slice(t * TILE, (t + 1) * TILE)
        schur_loads[t].wait()
        value = nt(scaled[...], schur[at, :])
        column = t * TILE + lax.broadcasted_iota(jnp.int32, value.shape, 1)
        value = jnp.where(column < live_size, value, 0.0)
        top = value.astype(jnp.bfloat16)
        rest = (value - top.astype(jnp.float32)).astype(jnp.bfloat16)
        image[:, at] = top
        total += nt(scaled[:, at], top) + nt(scaled[:, at], rest)
    image_out = pltpu.make_async_copy(image, image_h.at[0, 0], store_sem.at[1])
    image_out.start()
    part[:columns, :columns] = (total / interface).astype(jnp.bfloat16)

    picked = nn(row_pick[...], part[:columns, :])
    outgoing[...] = picked.astype(jnp.bfloat16).reshape(outgoing.shape)

    def far(step):
        peer = lax.rem(me + step, n_sub)
        return pltpu.make_async_remote_copy(
            src_ref=outgoing.at[peer],
            dst_ref=incoming.at[me],
            send_sem=far_send.at[step],
            recv_sem=far_recv.at[me],
            device_id={"sub": peer},
            device_id_type=MESH,
        )

    def send(step, carry):
        far(step).start()
        return carry

    lax.fori_loop(1, n_sub, send, 0)

    def high(i, carry):
        row = jnp.concatenate([cmap[pl.ds(i, 1), :], pad], axis=1)
        at = pl.ds(pl.multiple_of(i * LANES, LANES), LANES)
        high_pick[:, at] = jnp.where(high_at == (row >> 7), 1.0, 0.0).astype(jnp.bfloat16)
        return carry

    lax.fori_loop(0, n_sub, high, 0)

    def arrive(step, carry):
        source = lax.rem(me + step, n_sub)
        pltpu.make_async_copy(
            incoming.at[source], incoming.at[source], far_recv.at[source]
        ).wait()
        return carry

    lax.fori_loop(1, n_sub, arrive, 0)
    incoming[pl.ds(me, 1)] = outgoing[pl.ds(me, 1)]

    def fan(i, carry):
        at = pl.ds(pl.multiple_of(i * LANES, LANES), LANES)
        block = incoming[i]
        for h in range(highs):
            spread[h * rows : (h + 1) * rows, at] = (
                block * high_pick[h * rows : (h + 1) * rows, at]
            )
        return carry

    lax.fori_loop(0, n_sub, fan, 0)
    summed = nt(spread[...], low_pick[...])
    for h in range(highs):
        coarse[:, h * LANES : (h + 1) * LANES] = summed[h * rows : (h + 1) * rows, :]
    coarse_out = pltpu.make_async_copy(coarse, coarse_h.at[0], store_sem.at[2])
    coarse_out.start()

    def drain(step, carry):
        far(step).wait_send()
        return carry

    lax.fori_loop(1, n_sub, drain, 0)
    weights_out.wait()
    image_out.wait()
    coarse_out.wait()


def solution(mesh):
    n_sub, n_grp = mesh.shape["sub"], mesh.shape["grp"]

    def shards(
        interface_values, send_blocks, recv_blocks, block_counts, live_sizes, schur, basis, coarse_map
    ):
        blocks, width = interface_values.shape[2:]
        slots = send_blocks.shape[3]
        interface = schur.shape[2]
        columns = basis.shape[2]
        rows = 16
        section = rows * n_sub
        highs = section // LANES
        f32, bf16, i32 = jnp.float32, jnp.bfloat16, jnp.int32
        smem = pl.BlockSpec(memory_space=pltpu.SMEM)
        anywhere = pl.BlockSpec(memory_space=pl.ANY)
        return pl.pallas_call(
            functools.partial(kernel, n_sub, n_grp),
            out_shape=(
                jax.ShapeDtypeStruct((1, 1, blocks, width), f32),
                jax.ShapeDtypeStruct((1, 1, columns, interface), bf16),
                jax.ShapeDtypeStruct((1, rows, section), f32),
            ),
            in_specs=[smem] * 4 + [anywhere] * 4,
            out_specs=(anywhere,) * 3,
            scratch_shapes=[
                pltpu.VMEM((blocks, width), f32),
                pltpu.VMEM((columns, interface), bf16),
                pltpu.VMEM((interface, interface), bf16),
                pltpu.VMEM((n_sub, columns), i32),
                pltpu.VMEM((4, slots, width), f32),
                pltpu.VMEM((4, slots, width), f32),
                pltpu.VMEM((blocks, width), f32),
                pltpu.VMEM((columns, interface), bf16),
                pltpu.VMEM((columns, interface), bf16),
                pltpu.VMEM((LANES, LANES), bf16),
                pltpu.VMEM((section, columns), bf16),
                pltpu.VMEM((n_sub, rows, LANES), bf16),
                pltpu.VMEM((n_sub, rows, LANES), bf16),
                pltpu.VMEM((highs * rows, n_sub * LANES), bf16),
                pltpu.VMEM((LANES, n_sub * LANES), bf16),
                pltpu.VMEM((highs * rows, n_sub * LANES), bf16),
                pltpu.VMEM((rows, section), f32),
                pltpu.SemaphoreType.DMA((3,)),
                pltpu.SemaphoreType.DMA((interface // TILE,)),
                pltpu.SemaphoreType.DMA((3,)),
                pltpu.SemaphoreType.DMA((4,)),
                pltpu.SemaphoreType.DMA((4,)),
                pltpu.SemaphoreType.DMA((n_sub,)),
                pltpu.SemaphoreType.DMA((n_sub,)),
            ],
            compiler_params=pltpu.CompilerParams(
                collective_id=0, has_side_effects=True, vmem_limit_bytes=48 * 1024 * 1024
            ),
        )(
            send_blocks,
            recv_blocks,
            block_counts,
            live_sizes,
            interface_values,
            schur,
            basis,
            coarse_map,
        )

    placed = (
        P("grp", "sub", None, None),
        P("grp", "sub", None, None),
        P("grp", "sub", None, None),
        P("grp", "sub", None),
        P("grp", "sub"),
        P("grp", "sub", None, None),
        P("grp", "sub", None, None),
        P("grp", None, None),
    )
    return jax.shard_map(
        shards,
        mesh=mesh,
        in_specs=placed,
        out_specs=(P("grp", "sub", None, None), P("grp", "sub", None, None), P("grp", "sub", None)),
        check_vma=False,
    )
```

time: 186 us -> 42.6 us (0.23)
  the two profiles are of different devices: /device:TPU:2 before, /device:TPU:1 now
where the time goes in v1:
time: 42.6 us; the launch traced here: 42.3 us
  Pallas kernels  34.6 us (81%)
  local copies, waits for them, and re-layouts  6.43 us (15%)
  between operations  1.3 us (3%)
    pallas_call x1, Pallas kernels, shards(): pl.pallas_call(functools.partial(kernel, n_sub, n_grp), out_shape=(jax.Sh...  34.6 us
    unnamed x15, local copies, waits for them, and re-layouts  6.43 us

profile of v1, /device:TPU:1, one launch (start us, length us, event | category | flops | bytes accessed | tf_op | source)
XLA Modules:
  0.0 42.3 jit_solution(11939978904718581702)
XLA Ops:
  1.3 0.0 copy-start
  1.3 1.0 %copy-done = bf16[1,1,96,2048]{3,2,1,0:T(8,128)(2,1)S(1)} copy-done((bf16[1,1,96,2048]{3,2,1,0:T(8,128)(2,1)S(1)}, bf16[1,1,96,2048]{3,2,1,0:T(8,128)(2,1)}, u32[]{:S(2)}) %copy-start) | copy-done | bytes 393240
  2.3 0.0 copy-start.1
  2.3 0.8 %copy-done.1 = s32[1,64,96]{2,1,0:T(8,128)S(1)} copy-done((s32[1,64,96]{2,1,0:T(8,128)S(1)}, s32[1,64,96]{2,1,0:T(8,128)}, u32[]{:S(2)}) %copy-start.1) | copy-done | bytes 24600
  3.0 0.0 copy-start.2
  3.0 0.7 %copy-done.2 = f32[1,1,16,128]{3,2,1,0:T(8,128)S(1)} copy-done((f32[1,1,16,128]{3,2,1,0:T(8,128)S(1)}, f32[1,1,16,128]{3,2,1,0:T(8,128)}, u32[]{:S(2)}) %copy-start.2) | copy-done | bytes 8216
  3.7 0.0 copy-start.3
  3.7 0.7 %copy-done.3 = s32[1,1,4,8]{3,2,1,0:T(4,128)S(1)} copy-done((s32[1,1,4,8]{3,2,1,0:T(4,128)S(1)}, s32[1,1,4,8]{3,2,1,0:T(4,128)}, u32[]{:S(2)}) %copy-start.3) | copy-done | bytes 152
  4.4 0.0 copy-start.4
  4.4 0.7 %copy-done.4 = s32[1,1,4,8]{3,2,1,0:T(4,128)S(1)} copy-done((s32[1,1,4,8]{3,2,1,0:T(4,128)S(1)}, s32[1,1,4,8]{3,2,1,0:T(4,128)}, u32[]{:S(2)}) %copy-start.4) | copy-done | bytes 152
  5.1 0.0 copy-start.5
  5.1 0.7 %copy-done.5 = s32[1,1,4]{2,1,0:T(1,128)S(1)} copy-done((s32[1,1,4]{2,1,0:T(1,128)S(1)}, s32[1,1,4]{2,1,0:T(1,128)}, u32[]{:S(2)}) %copy-start.5) | copy-done | bytes 40
  5.8 34.6 %shard_map.103 = (f32[1,1,16,128]{3,2,1,0:T(8,128)S(1)}, bf16[1,1,96,2048]{3,2,1,0:T(8,128)(2,1)S(1)}, f32[1,16,1024]{2,1,0:T(8,128)S(1)}) custom-call(s32[1,1,4,8]{3,2,1,0:T(4,128)S(1)} %copy-done.3, s32[1,1,4,8]{3,2,1,0:T(4,128)S(1)} %copy-done.4, s32[1,1,4]{2,1,0:T(1,128)S(1)} %copy-done.5, s32[1,1]{1,0:T(1,128)S(6)} %copy.14.live_s, ...), custom_call_target="tpu_custom_call" | custom-call | tf_op jit(solution)/shard_map/pallas_call | solution.py:275
  40.3 0.6 %copy.15 = f32[1,1,16,128]{3,2,1,0:T(8,128)} copy(f32[1,1,16,128]{3,2,1,0:T(8,128)S(1)} %get-tuple-element.6) | data formatting | bytes 16384
  40.9 0.7 %copy.16 = bf16[1,1,96,2048]{3,2,1,0:T(8,128)(2,1)} copy(bf16[1,1,96,2048]{3,2,1,0:T(8,128)(2,1)S(1)} %get-tuple-element.7) | data formatting | bytes 786432
  41.7 0.6 %copy.17 = f32[1,16,1024]{2,1,0:T(8,128)} copy(f32[1,16,1024]{2,1,0:T(8,128)S(1)} %get-tuple-element.8) | data formatting | bytes 131072
Async XLA Ops:
  1.3 1.0 %copy-start = (bf16[1,1,96,2048]{3,2,1,0:T(8,128)(2,1)S(1)}, bf16[1,1,96,2048]{3,2,1,0:T(8,128)(2,1)}, u32[]{:S(2)}) copy-start(bf16[1,1,96,2048]{3,2,1,0:T(8,128)(2,1)} %basis_h.1) | copy-start | bytes 1179652
  2.3 0.8 %copy-start.1 = (s32[1,64,96]{2,1,0:T(8,128)S(1)}, s32[1,64,96]{2,1,0:T(8,128)}, u32[]{:S(2)}) copy-start(s32[1,64,96]{2,1,0:T(8,128)} %map_h.1) | copy-start | bytes 73732
  3.0 0.7 %copy-start.2 = (f32[1,1,16,128]{3,2,1,0:T(8,128)S(1)}, f32[1,1,16,128]{3,2,1,0:T(8,128)}, u32[]{:S(2)}) copy-start(f32[1,1,16,128]{3,2,1,0:T(8,128)} %values_h.1) | copy-start | bytes 24580
  3.7 0.7 %copy-start.3 = (s32[1,1,4,8]{3,2,1,0:T(4,128)S(1)}, s32[1,1,4,8]{3,2,1,0:T(4,128)}, u32[]{:S(2)}) copy-start(s32[1,1,4,8]{3,2,1,0:T(4,128)} %send_s.1) | copy-start | bytes 388
  4.4 0.7 %copy-start.4 = (s32[1,1,4,8]{3,2,1,0:T(4,128)S(1)}, s32[1,1,4,8]{3,2,1,0:T(4,128)}, u32[]{:S(2)}) copy-start(s32[1,1,4,8]{3,2,1,0:T(4,128)} %recv_s.1) | copy-start | bytes 388
  5.1 0.7 %copy-start.5 = (s32[1,1,4]{2,1,0:T(1,128)S(1)}, s32[1,1,4]{2,1,0:T(1,128)}, u32[]{:S(2)}) copy-start(s32[1,1,4]{2,1,0:T(1,128)} %counts_s.1) | copy-start | bytes 52

commit v2 on v0

v2 whole, which is shorter than its diff:
```python
import functools

import jax
import jax.numpy as jnp
from jax import lax
from jax.experimental import pallas as pl
from jax.experimental.pallas import tpu as pltpu
from jax.sharding import PartitionSpec as P

MESH = pl.DeviceIdType.MESH
LANES = 128
TILE = 256
POOL = 4


def nt(left, right):
    return lax.dot_general(
        left, right, (((1,), (1,)), ((), ())), preferred_element_type=jnp.float32
    )


def nn(left, right):
    return lax.dot_general(
        left, right, (((1,), (0,)), ((), ())), preferred_element_type=jnp.float32
    )


def exchange(
    n_sub,
    n_grp,
    live_s,
    send_h,
    recv_h,
    counts_h,
    values_h,
    schur_h,
    basis_h,
    map_h,
    weights,
    image,
    incoming,
    high_pick,
    low_pick,
    send_s,
    recv_s,
    counts_s,
    values,
    basis,
    schur,
    cmap,
    maps,
    packed,
    arrived,
    scaled,
    part,
    pool,
    terms,
    row_pick,
    outgoing,
    load_sem,
    schur_sem,
    near_send,
    near_recv,
    pool_send,
    pool_recv,
    far_send,
    far_recv,
):
    me = lax.axis_index("sub")
    group = lax.axis_index("grp")
    n_line = n_sub // POOL
    plane, place = me // n_line, lax.rem(me, n_line)
    interface = schur.shape[0]
    columns = basis.shape[0]
    blocks = values.shape[0]
    rows = incoming.shape[1]
    section = rows * n_sub
    highs = section // LANES
    slots = packed.shape[1]

    with jax.named_scope("start_loads"):
        pairs = [
            (values_h.at[0, 0], values),
            (send_h.at[0, 0], send_s),
            (counts_h.at[0], counts_s),
            (recv_h.at[0, 0], recv_s),
            (map_h.at[0], cmap),
            (basis_h.at[0, 0], basis),
        ]
        loads = [
            pltpu.make_async_copy(source, target, load_sem.at[i])
            for i, (source, target) in enumerate(pairs)
        ]
        for load in loads:
            load.start()
        tiles = interface // TILE
        schur_loads = [
            pltpu.make_async_copy(
                schur_h.at[0, 0, pl.ds(t * TILE, TILE)],
                schur.at[pl.ds(t * TILE, TILE)],
                schur_sem.at[t],
            )
            for t in range(tiles)
        ]
        for load in schur_loads:
            load.start()

    up = lax.rem(group + 1, n_grp)
    down = lax.rem(group + n_grp - 1, n_grp)
    with jax.named_scope("greet"):
        barrier = pltpu.get_barrier_semaphore()
        pl.semaphore_signal(barrier, inc=1, device_id={"grp": up}, device_id_type=MESH)
        pl.semaphore_signal(barrier, inc=1, device_id={"grp": down}, device_id_type=MESH)

        def greet(peer):
            pl.semaphore_signal(barrier, inc=1, device_id={"sub": peer}, device_id_type=MESH)

        right = lax.rem(me + 1, n_sub)
        left = lax.rem(me + n_sub - 1, n_sub)
        greet(right)
        greet(left)
        for step in range(1, POOL):
            greet(lax.rem(me + step * n_line, n_sub))
        for step in range(1, n_line):
            greet(plane * n_line + lax.rem(place + step, n_line))

    with jax.named_scope("pack"):
        for load in loads[:3]:
            load.wait()
        for j in range(4):
            for f in range(slots):
                row = values[pl.ds(send_s[j, f], 1), :]
                packed[j, f : f + 1, :] = jnp.where(f < counts_s[0, j], row, 0.0)

    with jax.named_scope("barrier"):
        pl.semaphore_wait(barrier, 4 + (POOL - 1) + (n_line - 1))

    with jax.named_scope("near_send"):
        targets = [{"sub": right}, {"sub": left}, {"grp": up}, {"grp": down}]
        near = [
            pltpu.make_async_remote_copy(
                src_ref=packed.at[j],
                dst_ref=arrived.at[j],
                send_sem=near_send.at[j],
                recv_sem=near_recv.at[j],
                device_id=targets[j],
                device_id_type=MESH,
            )
            for j in range(4)
        ]
        for copy in near:
            copy.start()

    with jax.named_scope("picks"):
        loads[4].wait()
        wide = POOL * columns
        line_map = jnp.concatenate(
            [cmap[k * n_line : (k + 1) * n_line, :] for k in range(POOL)], axis=1
        )
        maps[...] = line_map
        mine = maps[pl.ds(place, 1), :]
        own_rows = rows * n_line
        row_at = own_rows * plane + lax.broadcasted_iota(jnp.int32, (own_rows, wide), 0)
        row_pick[...] = jnp.where(row_at == mine, 1.0, 0.0).astype(jnp.bfloat16)
        low_at = lax.broadcasted_iota(jnp.int32, (LANES, wide), 0)
        high_at = lax.broadcasted_iota(jnp.int32, (highs * rows, wide), 0) // rows

        def low(i, carry):
            row = maps[pl.ds(i, 1), :]
            at = pl.ds(pl.multiple_of(i * wide, LANES), wide)
            low_pick[:, at] = jnp.where(low_at == (row & (LANES - 1)), 1.0, 0.0).astype(
                jnp.bfloat16
            )
            return carry

        lax.fori_loop(0, n_line, low, 0)
        terms[...] = jnp.zeros_like(terms)

    with jax.named_scope("near_wait"):
        for copy in near:
            copy.wait()
    with jax.named_scope("weights"):
        loads[3].wait()
        own = values[...]
        totals = own
        block_at = lax.broadcasted_iota(jnp.int32, own.shape, 0)
        for j in range(4):
            came = arrived[j]
            if j == 2:
                came = jnp.where(group > 0, came, 0.0)
            if j == 3:
                came = jnp.where(group < n_grp - 1, came, 0.0)
            for f in range(slots):
                totals += jnp.where(block_at == recv_s[j, f], came[f : f + 1, :], 0.0)
        weight = own / totals
        weights[0, 0] = weight

        live_size = live_s[0, 0]
        unknown = block_at * LANES + lax.broadcasted_iota(jnp.int32, own.shape, 1)
        live_weight = jnp.where(unknown < live_size, weight, 0.0)
    with jax.named_scope("scaled"):
        loads[5].wait()
        for n in range(blocks):
            at = slice(n * LANES, (n + 1) * LANES)
            scaled[:, at] = (basis[:, at].astype(jnp.float32) * live_weight[n : n + 1, :]).astype(
                jnp.bfloat16
            )

    with jax.named_scope("schur_wait"):
        for load in schur_loads:
            load.wait()
    with jax.named_scope("image"):
        total = jnp.zeros((columns, columns), jnp.float32)
        for t in range(tiles):
            at = slice(t * TILE, (t + 1) * TILE)
            value = nt(scaled[...], schur[at, :])
            column = t * TILE + lax.broadcasted_iota(jnp.int32, value.shape, 1)
            value = jnp.where(column < live_size, value, 0.0)
            top = value.astype(jnp.bfloat16)
            rest = (value - top.astype(jnp.float32)).astype(jnp.bfloat16)
            image[0, 0, :, at] = top
            total += nt(scaled[:, at], top) + nt(scaled[:, at], rest)
    with jax.named_scope("part"):
        value = jnp.concatenate(
            [total / interface, jnp.zeros((columns, LANES - columns), jnp.float32)], axis=1
        )
        part[...] = pltpu.roll(value, lax.rem(columns * plane, LANES), 1).astype(jnp.bfloat16)

    with jax.named_scope("pool_send"):
        shared = []
        for step in range(1, POOL):
            other = lax.rem(plane + step, POOL)
            copy = pltpu.make_async_remote_copy(
                src_ref=part,
                dst_ref=pool.at[plane],
                send_sem=pool_send.at[step],
                recv_sem=pool_recv.at[plane],
                device_id={"sub": other * n_line + place},
                device_id_type=MESH,
            )
            copy.start()
            shared.append(copy)
    with jax.named_scope("pool_wait"):
        for step in range(1, POOL):
            other = lax.rem(plane + step, POOL)
            pltpu.make_async_copy(pool.at[other], pool.at[other], pool_recv.at[other]).wait()
        pool[pl.ds(plane, 1)] = part[...][None]
    with jax.named_scope("pick_rows"):
        lane = lax.broadcasted_iota(jnp.int32, (columns, LANES), 1)
        for k in range(POOL):
            first, last = k * columns, (k + 1) * columns
            for t in range(first // LANES, (last - 1) // LANES + 1):
                inside = (lane + t * LANES >= first) & (lane + t * LANES < last)
                keep = jnp.where(inside, 1.0, 0.0).astype(jnp.bfloat16)
                terms[first:last, t * LANES : (t + 1) * LANES] = pool[k] * keep
        picked = nn(row_pick[...], terms[...])
        outgoing[...] = picked.astype(jnp.bfloat16).reshape(outgoing.shape)

    def far(step):
        peer = lax.rem(place + step, n_line)
        return pltpu.make_async_remote_copy(
            src_ref=outgoing.at[peer],
            dst_ref=incoming.at[place],
            send_sem=far_send.at[step],
            recv_sem=far_recv.at[place],
            device_id={"sub": plane * n_line + peer},
            device_id_type=MESH,
        )

    with jax.named_scope("far_send"):
        sent = [far(step) for step in range(1, n_line)]
        for copy in sent:
            copy.start()

    def high(i, carry):
        row = maps[pl.ds(i, 1), :]
        at = pl.ds(pl.multiple_of(i * wide, LANES), wide)
        high_pick[:, at] = jnp.where(high_at == (row >> 7), 1.0, 0.0).astype(jnp.bfloat16)
        return carry

    with jax.named_scope("high"):
        lax.fori_loop(0, n_line, high, 0)
    with jax.named_scope("arrive"):
        for step in range(1, n_line):
            source = lax.rem(place + n_line - step, n_line)
            pltpu.make_async_copy(
                incoming.at[source], incoming.at[source], far_recv.at[source]
            ).wait()
        incoming[pl.ds(place, 1)] = outgoing[pl.ds(place, 1)]
    with jax.named_scope("drain"):
        for copy in shared + sent:
            copy.wait_send()


def assemble(
    weights,
    image,
    incoming,
    high_pick,
    low_pick,
    weights_h,
    image_h,
    coarse_h,
    spread,
    coarse,
    store_sem,
):
    rows = incoming.shape[1]
    n_line, _, wide = incoming.shape
    highs = high_pick.shape[0] // rows
    weights_out = pltpu.make_async_copy(weights, weights_h, store_sem.at[0])
    weights_out.start()
    image_out = pltpu.make_async_copy(image, image_h, store_sem.at[1])
    image_out.start()

    def fan(i, carry):
        at = pl.ds(pl.multiple_of(i * wide, LANES), wide)
        block = incoming[i]
        for h in range(highs):
            spread[h * rows : (h + 1) * rows, at] = (
                block * high_pick[h * rows : (h + 1) * rows, at]
            )
        return carry

    with jax.named_scope("fan"):
        lax.fori_loop(0, n_line, fan, 0)
    with jax.named_scope("add"):
        summed = nt(spread[...], low_pick[...])
        for h in range(highs):
            coarse[0, :, h * LANES : (h + 1) * LANES] = summed[h * rows : (h + 1) * rows, :]
    with jax.named_scope("store"):
        coarse_out = pltpu.make_async_copy(coarse, coarse_h, store_sem.at[2])
        coarse_out.start()
        weights_out.wait()
        image_out.wait()
        coarse_out.wait()


def solution(mesh):
    n_sub, n_grp = mesh.shape["sub"], mesh.shape["grp"]

    def shards(
        interface_values, send_blocks, recv_blocks, block_counts, live_sizes, schur, basis, coarse_map
    ):
        blocks, width = interface_values.shape[2:]
        slots = send_blocks.shape[3]
        interface = schur.shape[2]
        columns = basis.shape[2]
        rows = 16
        section = rows * n_sub
        highs = section // LANES
        n_line = n_sub // POOL
        wide = POOL * columns
        f32, bf16, i32 = jnp.float32, jnp.bfloat16, jnp.int32
        hbm = pl.BlockSpec(memory_space=pltpu.HBM)
        vmem = pl.BlockSpec(memory_space=pltpu.VMEM)
        pinned = [
            pltpu.with_memory_space_constraint(x, pltpu.HBM)
            for x in (send_blocks, recv_blocks, block_counts, interface_values, schur, basis, coarse_map)
        ]
        made = pl.pallas_call(
            functools.partial(exchange, n_sub, n_grp),
            out_shape=(
                jax.ShapeDtypeStruct((1, 1, blocks, width), f32),
                jax.ShapeDtypeStruct((1, 1, columns, interface), bf16),
                jax.ShapeDtypeStruct((n_line, rows, wide), bf16),
                jax.ShapeDtypeStruct((highs * rows, n_line * wide), bf16),
                jax.ShapeDtypeStruct((LANES, n_line * wide), bf16),
            ),
            in_specs=[pl.BlockSpec(memory_space=pltpu.SMEM)] + [hbm] * 7,
            out_specs=(vmem,) * 5,
            scratch_shapes=[
                pltpu.SMEM((4, slots), i32),
                pltpu.SMEM((4, slots), i32),
                pltpu.SMEM((1, 4), i32),
                pltpu.VMEM((blocks, width), f32),
                pltpu.VMEM((columns, interface), bf16),
                pltpu.VMEM((interface, interface), bf16),
                pltpu.VMEM((n_sub, columns), i32),
                pltpu.VMEM((n_line, wide), i32),
                pltpu.VMEM((4, slots, width), f32),
                pltpu.VMEM((4, slots, width), f32),
                pltpu.VMEM((columns, interface), bf16),
                pltpu.VMEM((columns, LANES), bf16),
                pltpu.VMEM((POOL, columns, LANES), bf16),
                pltpu.VMEM((wide, wide), bf16),
                pltpu.VMEM((rows * n_line, wide), bf16),
                pltpu.VMEM((n_line, rows, wide), bf16),
                pltpu.SemaphoreType.DMA((6,)),
                pltpu.SemaphoreType.DMA((interface // TILE,)),
                pltpu.SemaphoreType.DMA((4,)),
                pltpu.SemaphoreType.DMA((4,)),
                pltpu.SemaphoreType.DMA((POOL,)),
                pltpu.SemaphoreType.DMA((POOL,)),
                pltpu.SemaphoreType.DMA((n_line,)),
                pltpu.SemaphoreType.DMA((n_line,)),
            ],
            compiler_params=pltpu.CompilerParams(
                collective_id=0, has_side_effects=True, vmem_limit_bytes=32 * 1024 * 1024
            ),
        )(live_sizes, *pinned)
        return pl.pallas_call(
            assemble,
            out_shape=(
                jax.ShapeDtypeStruct((1, 1, blocks, width), f32),
                jax.ShapeDtypeStruct((1, 1, columns, interface), bf16),
                jax.ShapeDtypeStruct((1, rows, section), f32),
            ),
            in_specs=[vmem] * 5,
            out_specs=(hbm,) * 3,
            scratch_shapes=[
                pltpu.VMEM((highs * rows, n_line * wide), bf16),
                pltpu.VMEM((1, rows, section), f32),
                pltpu.SemaphoreType.DMA((3,)),
            ],
            compiler_params=pltpu.CompilerParams(vmem_limit_bytes=16 * 1024 * 1024),
        )(*made)

    placed = (
        P("grp", "sub", None, None),
        P("grp", "sub", None, None),
        P("grp", "sub", None, None),
        P("grp", "sub", None),
        P("grp", "sub"),
        P("grp", "sub", None, None),
        P("grp", "sub", None, None),
        P("grp", None, None),
    )
    return jax.shard_map(
        shards,
        mesh=mesh,
        in_specs=placed,
        out_specs=(P("grp", "sub", None, None), P("grp", "sub", None, None), P("grp", "sub", None)),
        check_vma=False,
    )
```

time: 186 us -> 31.6 us (0.17)
  the two profiles are of different devices: /device:TPU:2 before, /device:TPU:1 now
where the time goes in v2:
time: 31.6 us; the launch traced here: 31.5 us
  Pallas kernels  30.2 us (96%)
  between operations  1.29 us (4%)
    pallas_call x1, Pallas kernels, shards(): pl.pallas_call(functools.partial(exchange, n_sub, n_grp), out_shape=(jax....  28.8 us
    pallas_call x1, Pallas kernels, shards(): pl.pallas_call(assemble, out_shape=(jax.ShapeDtypeStruct((1, 1, blocks, w...  1.46 us

profile of v2, /device:TPU:1, one launch (start us, length us, event | category | flops | bytes accessed | tf_op | source)
XLA Modules:
  0.0 31.5 jit_solution(17615738234379124146)
XLA Ops:
  1.3 28.8 %shard_map.103 = (f32[1,1,16,128]{3,2,1,0:T(8,128)S(1)}, bf16[1,1,96,2048]{3,2,1,0:T(8,128)(2,1)S(1)}, bf16[16,16,384]{2,1,0:T(8,128)(2,1)S(1)}, bf16[128,6144]{1,0:T(8,128)(2,1)S(1)}, bf16[128,6144]{1,0:T(8,128)(2,1)S(1)}) custom-call(s32[1,1]{1,0:T(1,128)S(6)} %copy.11.live_s, s32[1,1,4,8]{3,2,1,0:T(4,128)} %send_h.1, s32[1,1,4,8]{3,2,1,0:T(4,128)} %recv_h.1, ...), custom_call_target="tpu_custom_call" | custom-call | tf_op jit(solution)/shard_map/pallas_call | solution.py:361
  30.1 1.5 %shard_map.104 = (f32[1,1,16,128]{3,2,1,0:T(8,128)}, bf16[1,1,96,2048]{3,2,1,0:T(8,128)(2,1)}, f32[1,16,1024]{2,1,0:T(8,128)}) custom-call(f32[1,1,16,128]{3,2,1,0:T(8,128)S(1)} %get-tuple-element.8.weights, bf16[1,1,96,2048]{3,2,1,0:T(8,128)(2,1)S(1)} %get-tuple-element.9.image, bf16[16,16,384]{2,1,0:T(8,128)(2,1)S(1)} %get-tuple-element.10.incoming, ...), custom_call_target="tpu_custom_call" | custom-call | tf_op jit(solution)/shard_map/pallas_call | solution.py:402

commit v3 on v2

--- a/solution.py
+++ b/solution.py
@@ -9,7 +9,7 @@
 
 MESH = pl.DeviceIdType.MESH
 LANES = 128
-TILE = 256
+TILE = 512
 POOL = 4
 
 
@@ -51,7 +51,10 @@
     maps,
     packed,
     arrived,
+    basis_t,
+    scaled_t,
     scaled,
+    halves,
     part,
     pool,
     terms,
@@ -91,7 +94,30 @@
             pltpu.make_async_copy(source, target, load_sem.at[i])
             for i, (source, target) in enumerate(pairs)
         ]
-        for load in loads:
+        for load in loads[:3]:
+            load.start()
+
+    up = lax.rem(group + 1, n_grp)
+    down = lax.rem(group + n_grp - 1, n_grp)
+    right = lax.rem(me + 1, n_sub)
+    left = lax.rem(me + n_sub - 1, n_sub)
+    half = n_line // 2
+    distant = [half] + [s for i in range(1, half) for s in (half - i, half + i)]
+    with jax.named_scope("greet"):
+        barrier = pltpu.get_barrier_semaphore()
+
+        def greet(target):
+            pl.semaphore_signal(barrier, inc=1, device_id=target, device_id_type=MESH)
+
+        for step in distant:
+            greet({"sub": plane * n_line + lax.rem(place + step, n_line)})
+        for step in range(1, POOL):
+            greet({"sub": lax.rem(me + step * n_line, n_sub)})
+        for target in ({"sub": right}, {"sub": left}, {"grp": up}, {"grp": down}):
+            greet(target)
+
+    with jax.named_scope("start_more"):
+        for load in loads[3:]:
             load.start()
         tiles = interface // TILE
         schur_loads = [
@@ -104,25 +130,6 @@
         ]
         for load in schur_loads:
             load.start()
-
-    up = lax.rem(group + 1, n_grp)
-    down = lax.rem(group + n_grp - 1, n_grp)
-    with jax.named_scope("greet"):
-        barrier = pltpu.get_barrier_semaphore()
-        pl.semaphore_signal(barrier, inc=1, device_id={"grp": up}, device_id_type=MESH)
-        pl.semaphore_signal(barrier, inc=1, device_id={"grp": down}, device_id_type=MESH)
-
-        def greet(peer):
-            pl.semaphore_signal(barrier, inc=1, device_id={"sub": peer}, device_id_type=MESH)
-
-        right = lax.rem(me + 1, n_sub)
-        left = lax.rem(me + n_sub - 1, n_sub)
-        greet(right)
-        greet(left)
-        for step in range(1, POOL):
-            greet(lax.rem(me + step * n_line, n_sub))
-        for step in range(1, n_line):
-            greet(plane * n_line + lax.rem(place + step, n_line))
 
     with jax.named_scope("pack"):
         for load in loads[:3]:
@@ -175,6 +182,12 @@
 
         lax.fori_loop(0, n_line, low, 0)
         terms[...] = jnp.zeros_like(terms)
+
+    with jax.named_scope("turn_basis"):
+        loads[5].wait()
+        for n in range(blocks):
+            at = slice(n * LANES, (n + 1) * LANES)
+            basis_t[at, :] = basis[:, at].astype(jnp.float32).T
 
     with jax.named_scope("near_wait"):
         for copy in near:
@@ -199,9 +212,10 @@
         unknown = block_at * LANES + lax.broadcasted_iota(jnp.int32, own.shape, 1)
         live_weight = jnp.where(unknown < live_size, weight, 0.0)
     with jax.named_scope("scaled"):
-        loads[5].wait()
+        columns_of = live_weight.T
         for n in range(blocks):
             at = slice(n * LANES, (n + 1) * LANES)
+            scaled_t[at, :] = (basis_t[at, :] * columns_of[:, n : n + 1]).astype(jnp.bfloat16)
             scaled[:, at] = (basis[:, at].astype(jnp.float32) * live_weight[n : n + 1, :]).astype(
                 jnp.bfloat16
             )
@@ -210,17 +224,18 @@
         for load in schur_loads:
             load.wait()
     with jax.named_scope("image"):
-        total = jnp.zeros((columns, columns), jnp.float32)
         for t in range(tiles):
             at = slice(t * TILE, (t + 1) * TILE)
-            value = nt(scaled[...], schur[at, :])
-            column = t * TILE + lax.broadcasted_iota(jnp.int32, value.shape, 1)
-            value = jnp.where(column < live_size, value, 0.0)
+            value = nn(schur[at, :], scaled_t[...])
+            row = t * TILE + lax.broadcasted_iota(jnp.int32, value.shape, 0)
+            value = jnp.where(row < live_size, value, 0.0)
             top = value.astype(jnp.bfloat16)
             rest = (value - top.astype(jnp.float32)).astype(jnp.bfloat16)
-            image[0, 0, :, at] = top
-            total += nt(scaled[:, at], top) + nt(scaled[:, at], rest)
+            halves[at, :columns] = top
+            halves[at, LANES : LANES + columns] = rest
     with jax.named_scope("part"):
+        total = nn(scaled[...], halves[...])
+        total = total[:, :columns] + total[:, LANES:]
         value = jnp.concatenate(
             [total / interface, jnp.zeros((columns, LANES - columns), jnp.float32)], axis=1
         )
@@ -268,7 +283,7 @@
         )
 
     with jax.named_scope("far_send"):
-        sent = [far(step) for step in range(1, n_line)]
+        sent = [far(step) for step in distant]
         for copy in sent:
             copy.start()
 
@@ -280,6 +295,10 @@
 
     with jax.named_scope("high"):
         lax.fori_loop(0, n_line, high, 0)
+    with jax.named_scope("turn_image"):
+        for n in range(blocks):
+            at = slice(n * LANES, (n + 1) * LANES)
+            image[0, 0, :, at] = halves[at, :columns].astype(jnp.float32).T.astype(jnp.bfloat16)
     with jax.named_scope("arrive"):
         for step in range(1, n_line):
             source = lax.rem(place + n_line - step, n_line)
@@ -380,7 +399,10 @@
                 pltpu.VMEM((n_line, wide), i32),
                 pltpu.VMEM((4, slots, width), f32),
                 pltpu.VMEM((4, slots, width), f32),
+                pltpu.VMEM((interface, columns), f32),
+                pltpu.VMEM((interface, columns), bf16),
                 pltpu.VMEM((columns, interface), bf16),
+                pltpu.VMEM((interface, LANES + columns), bf16),
                 pltpu.VMEM((columns, LANES), bf16),
                 pltpu.VMEM((POOL, columns, LANES), bf16),
                 pltpu.VMEM((wide, wide), bf16),

time: 31.6 us -> 29.9 us (0.946)
  Pallas kernels: 30.2 us -> 28.4 us
    pallas_call x1, Pallas kernels: 28.8 us -> 27 us  [shards(): pl.pallas_call(functools.partial(exchange, n_sub, n_grp), out_shape=(jax....]
where the time goes in v3:
time: 29.9 us; the launch traced here: 29.7 us
  Pallas kernels  28.4 us (95%)
  between operations  1.29 us (4%)
    pallas_call x1, Pallas kernels, shards(): pl.pallas_call(functools.partial(exchange, n_sub, n_grp), out_shape=(jax....  27 us
    pallas_call x1, Pallas kernels, shards(): pl.pallas_call(assemble, out_shape=(jax.ShapeDtypeStruct((1, 1, blocks, w...  1.46 us

profile of v3, /device:TPU:1, one launch (start us, length us, event | category | flops | bytes accessed | tf_op | source)
XLA Modules:
  0.0 29.7 jit_solution(7960324357408182592)
XLA Ops:
  1.3 27.0 %shard_map.103 = (f32[1,1,16,128]{3,2,1,0:T(8,128)S(1)}, bf16[1,1,96,2048]{3,2,1,0:T(8,128)(2,1)S(1)}, bf16[16,16,384]{2,1,0:T(8,128)(2,1)S(1)}, bf16[128,6144]{1,0:T(8,128)(2,1)S(1)}, bf16[128,6144]{1,0:T(8,128)(2,1)S(1)}) custom-call(s32[1,1]{1,0:T(1,128)S(6)} %copy.11.live_s, s32[1,1,4,8]{3,2,1,0:T(4,128)} %send_h.1, s32[1,1,4,8]{3,2,1,0:T(4,128)} %recv_h.1, ...), custom_call_target="tpu_custom_call" | custom-call | tf_op jit(solution)/shard_map/pallas_call | solution.py:380
  28.3 1.5 %shard_map.104 = (f32[1,1,16,128]{3,2,1,0:T(8,128)}, bf16[1,1,96,2048]{3,2,1,0:T(8,128)(2,1)}, f32[1,16,1024]{2,1,0:T(8,128)}) custom-call(f32[1,1,16,128]{3,2,1,0:T(8,128)S(1)} %get-tuple-element.8.weights, bf16[1,1,96,2048]{3,2,1,0:T(8,128)(2,1)S(1)} %get-tuple-element.9.image, bf16[16,16,384]{2,1,0:T(8,128)(2,1)S(1)} %get-tuple-element.10.incoming, ...), custom_call_target="tpu_custom_call" | custom-call | tf_op jit(solution)/shard_map/pallas_call | solution.py:424

commit v4 on v3

--- a/solution.py
+++ b/solution.py
@@ -101,8 +101,10 @@
     down = lax.rem(group + n_grp - 1, n_grp)
     right = lax.rem(me + 1, n_sub)
     left = lax.rem(me + n_sub - 1, n_sub)
-    half = n_line // 2
-    distant = [half] + [s for i in range(1, half) for s in (half - i, half + i)]
+    apart = [min(step, n_line - step) for step in range(n_line)]
+    distant = sorted(
+        range(1, n_line), key=lambda step: (-((apart[step] + 1) // 2), -(apart[step] % 2))
+    )
     with jax.named_scope("greet"):
         barrier = pltpu.get_barrier_semaphore()
 
@@ -216,15 +218,17 @@
         for n in range(blocks):
             at = slice(n * LANES, (n + 1) * LANES)
             scaled_t[at, :] = (basis_t[at, :] * columns_of[:, n : n + 1]).astype(jnp.bfloat16)
-            scaled[:, at] = (basis[:, at].astype(jnp.float32) * live_weight[n : n + 1, :]).astype(
-                jnp.bfloat16
-            )
 
     with jax.named_scope("schur_wait"):
         for load in schur_loads:
             load.wait()
     with jax.named_scope("image"):
         for t in range(tiles):
+            for n in range(t * TILE // LANES, (t + 1) * TILE // LANES):
+                at = slice(n * LANES, (n + 1) * LANES)
+                scaled[:, at] = (
+                    basis[:, at].astype(jnp.float32) * live_weight[n : n + 1, :]
+                ).astype(jnp.bfloat16)
             at = slice(t * TILE, (t + 1) * TILE)
             value = nn(schur[at, :], scaled_t[...])
             row = t * TILE + lax.broadcasted_iota(jnp.int32, value.shape, 0)
@@ -243,7 +247,7 @@
 
     with jax.named_scope("pool_send"):
         shared = []
-        for step in range(1, POOL):
+        for step in sorted(range(1, POOL), key=lambda step: -min(step, POOL - step)):
             other = lax.rem(plane + step, POOL)
             copy = pltpu.make_async_remote_copy(
                 src_ref=part,
@@ -333,7 +337,7 @@
     image_out.start()
 
     def fan(i, carry):
-        at = pl.ds(pl.multiple_of(i * wide, LANES), wide)
+        at = slice(i * wide, (i + 1) * wide)
         block = incoming[i]
         for h in range(highs):
             spread[h * rows : (h + 1) * rows, at] = (
@@ -342,7 +346,8 @@
         return carry
 
     with jax.named_scope("fan"):
-        lax.fori_loop(0, n_line, fan, 0)
+        for i in range(n_line):
+            fan(i, 0)
     with jax.named_scope("add"):
         summed = nt(spread[...], low_pick[...])
         for h in range(highs):

time: 29.9 us -> 29.5 us (0.987)
  Pallas kernels: 28.4 us -> 28.1 us
where the time goes in v4:
time: 29.5 us; the launch traced here: 29.4 us
  Pallas kernels  28.1 us (95%)
  between operations  1.29 us (4%)
    pallas_call x1, Pallas kernels, shards(): pl.pallas_call(functools.partial(exchange, n_sub, n_grp), out_shape=(jax....  26.8 us
    pallas_call x1, Pallas kernels, shards(): pl.pallas_call(assemble, out_shape=(jax.ShapeDtypeStruct((1, 1, blocks, w...  1.29 us

profile of v4, /device:TPU:1, one launch (start us, length us, event | category | flops | bytes accessed | tf_op | source)
XLA Modules:
  0.0 29.4 jit_solution(12206014489715853611)
XLA Ops:
  1.3 26.8 %shard_map.103 = (f32[1,1,16,128]{3,2,1,0:T(8,128)S(1)}, bf16[1,1,96,2048]{3,2,1,0:T(8,128)(2,1)S(1)}, bf16[16,16,384]{2,1,0:T(8,128)(2,1)S(1)}, bf16[128,6144]{1,0:T(8,128)(2,1)S(1)}, bf16[128,6144]{1,0:T(8,128)(2,1)S(1)}) custom-call(s32[1,1]{1,0:T(1,128)S(6)} %copy.11.live_s, s32[1,1,4,8]{3,2,1,0:T(4,128)} %send_h.1, s32[1,1,4,8]{3,2,1,0:T(4,128)} %recv_h.1, ...), custom_call_target="tpu_custom_call" | custom-call | tf_op jit(solution)/shard_map/pallas_call | solution.py:385
  28.1 1.3 %shard_map.104 = (f32[1,1,16,128]{3,2,1,0:T(8,128)}, bf16[1,1,96,2048]{3,2,1,0:T(8,128)(2,1)}, f32[1,16,1024]{2,1,0:T(8,128)}) custom-call(f32[1,1,16,128]{3,2,1,0:T(8,128)S(1)} %get-tuple-element.8.weights, bf16[1,1,96,2048]{3,2,1,0:T(8,128)(2,1)S(1)} %get-tuple-element.9.image, bf16[16,16,384]{2,1,0:T(8,128)(2,1)S(1)} %get-tuple-element.10.incoming, ...), custom_call_target="tpu_custom_call" | custom-call | tf_op jit(solution)/shard_map/pallas_call | solution.py:429

commit v5 on v4

--- a/solution.py
+++ b/solution.py
@@ -168,9 +168,12 @@
         )
         maps[...] = line_map
         mine = maps[pl.ds(place, 1), :]
-        own_rows = rows * n_line
-        row_at = own_rows * plane + lax.broadcasted_iota(jnp.int32, (own_rows, wide), 0)
-        row_pick[...] = jnp.where(row_at == mine, 1.0, 0.0).astype(jnp.bfloat16)
+        row_at = lax.broadcasted_iota(jnp.int32, (rows, wide), 0)
+        for i, step in enumerate(distant + [0]):
+            owner = plane * n_line + lax.rem(place + step, n_line)
+            row_pick[i * rows : (i + 1) * rows, :] = jnp.where(
+                row_at == mine - rows * owner, 1.0, 0.0
+            ).astype(jnp.bfloat16)
         low_at = lax.broadcasted_iota(jnp.int32, (LANES, wide), 0)
         high_at = lax.broadcasted_iota(jnp.int32, (highs * rows, wide), 0) // rows
 
@@ -241,7 +244,7 @@
         total = nn(scaled[...], halves[...])
         total = total[:, :columns] + total[:, LANES:]
         value = jnp.concatenate(
-            [total / interface, jnp.zeros((columns, LANES - columns), jnp.float32)], axis=1
+            [total * (1.0 / interface), jnp.zeros((columns, LANES - columns), jnp.float32)], axis=1
         )
         part[...] = pltpu.roll(value, lax.rem(columns * plane, LANES), 1).astype(jnp.bfloat16)
 
@@ -272,24 +275,28 @@
                 inside = (lane + t * LANES >= first) & (lane + t * LANES < last)
                 keep = jnp.where(inside, 1.0, 0.0).astype(jnp.bfloat16)
                 terms[first:last, t * LANES : (t + 1) * LANES] = pool[k] * keep
-        picked = nn(row_pick[...], terms[...])
-        outgoing[...] = picked.astype(jnp.bfloat16).reshape(outgoing.shape)
-
-    def far(step):
+
+    def far(i, step):
         peer = lax.rem(place + step, n_line)
         return pltpu.make_async_remote_copy(
-            src_ref=outgoing.at[peer],
+            src_ref=outgoing.at[i],
             dst_ref=incoming.at[place],
-            send_sem=far_send.at[step],
+            send_sem=far_send.at[i],
             recv_sem=far_recv.at[place],
             device_id={"sub": plane * n_line + peer},
             device_id_type=MESH,
         )
 
-    with jax.named_scope("far_send"):
-        sent = [far(step) for step in distant]
-        for copy in sent:
-            copy.start()
+    sent = []
+    half = n_line // 2
+    for first in (0, half):
+        with jax.named_scope("pick_rows"):
+            picked = nn(row_pick[first * rows : (first + half) * rows, :], terms[...])
+            outgoing[first : first + half] = picked.astype(jnp.bfloat16).reshape(half, rows, wide)
+        with jax.named_scope("far_send"):
+            for i in range(first, min(first + half, n_line - 1)):
+                sent.append(far(i, distant[i]))
+                sent[-1].start()
 
     def high(i, carry):
         row = maps[pl.ds(i, 1), :]
@@ -309,7 +316,7 @@
             pltpu.make_async_copy(
                 incoming.at[source], incoming.at[source], far_recv.at[source]
             ).wait()
-        incoming[pl.ds(place, 1)] = outgoing[pl.ds(place, 1)]
+        incoming[pl.ds(place, 1)] = outgoing[n_line - 1 : n_line]
     with jax.named_scope("drain"):
         for copy in shared + sent:
             copy.wait_send()

time: 29.5 us -> 29.4 us (level)
  no operation moved by 1% of the time
where the time goes in v5:
time: 29.4 us; the launch traced here: 29.3 us
  Pallas kernels  28 us (95%)
  between operations  1.29 us (4%)
    pallas_call x1, Pallas kernels, shards(): pl.pallas_call(functools.partial(exchange, n_sub, n_grp), out_shape=(jax....  26.7 us
    pallas_call x1, Pallas kernels, shards(): pl.pallas_call(assemble, out_shape=(jax.ShapeDtypeStruct((1, 1, blocks, w...  1.29 us

profile of v5, /device:TPU:1, one launch (start us, length us, event | category | flops | bytes accessed | tf_op | source)
XLA Modules:
  0.0 29.3 jit_solution(9900151330846024474)
XLA Ops:
  1.3 26.7 %shard_map.103 = (f32[1,1,16,128]{3,2,1,0:T(8,128)S(1)}, bf16[1,1,96,2048]{3,2,1,0:T(8,128)(2,1)S(1)}, bf16[16,16,384]{2,1,0:T(8,128)(2,1)S(1)}, bf16[128,6144]{1,0:T(8,128)(2,1)S(1)}, bf16[128,6144]{1,0:T(8,128)(2,1)S(1)}) custom-call(s32[1,1]{1,0:T(1,128)S(6)} %copy.11.live_s, s32[1,1,4,8]{3,2,1,0:T(4,128)} %send_h.1, s32[1,1,4,8]{3,2,1,0:T(4,128)} %recv_h.1, ...), custom_call_target="tpu_custom_call" | custom-call | tf_op jit(solution)/shard_map/pallas_call | solution.py:392
  28.0 1.3 %shard_map.104 = (f32[1,1,16,128]{3,2,1,0:T(8,128)}, bf16[1,1,96,2048]{3,2,1,0:T(8,128)(2,1)}, f32[1,16,1024]{2,1,0:T(8,128)}) custom-call(f32[1,1,16,128]{3,2,1,0:T(8,128)S(1)} %get-tuple-element.8.weights, bf16[1,1,96,2048]{3,2,1,0:T(8,128)(2,1)S(1)} %get-tuple-element.9.image, bf16[16,16,384]{2,1,0:T(8,128)(2,1)S(1)} %get-tuple-element.10.incoming, ...), custom_call_target="tpu_custom_call" | custom-call | tf_op jit(solution)/shard_map/pallas_call | solution.py:436
